TPU v7x, 256 devices: a whole 4x4x8 slice. The times are simulated.
256 devices in a mesh: gx: 16 (over y, x), gy: 16 (over z, core).
Axes of the slice: x: 4, y: 4, z: 8, core: 2. Of those that a mesh axis runs over, the one named last changes fastest.
Arguments:
- pressure: float32 [2, 2048, 2048], P(None, 'gx', 'gy'), may hold values from 0.5 to 1.5
- saturations: float32 [2, 2, 2048, 2048], P(None, None, 'gx', 'gy'), may hold values from 0.05 to 0.4
- old_mass: float32 [3, 2, 2048, 2048], P(None, None, 'gx', 'gy'), may hold values from 0 to 0.4
- pore_volume: float32 [2, 2048, 2048], P(None, 'gx', 'gy'), may hold values from 0.3 to 3
- transmissibility: float32 [3, 2, 2048, 2048], P(None, None, 'gx', 'gy'), may hold values from 0.3 to 3
- direction: float32 [3, 2, 2048, 2048], P(None, None, 'gx', 'gy'), may hold values from -6 to 6
- seg_pressure: float32 [512, 128], P('gx'), may hold values from 0.4 to 1.2
- seg_direction: float32 [512, 128], P('gx'), may hold values from -6 to 6
- perf_cell: int32 [512, 128], P('gx'), may hold values from 0 to 524287, as said below
- well_index: float32 [512, 128], P('gx'), may hold values from 0.2 to 2
- parent: int32 [512, 128], P('gx'), may hold values from 0 to 126, as said below
- seg_head: float32 [512, 128], P('gx'), may hold values from 0 to 0.3
- well_mode: int32 [512], P('gx'), may hold values from 0 to 1
- bhp_limit: float32 [512], P('gx'), may hold values from 0.3 to 0.8
- guide_rate: float32 [512], P('gx'), may hold values from 0.5 to 5
- group_of: int32 [512, 1], P('gx'), may hold values from 0 to 127
- group_target: float32 [128], replicated, may hold values from 200 to 800
Outputs:
- cell_residual: float32 [3, 2, 2048, 2048], P(None, None, 'gx', 'gy')
- cell_jvp: float32 [3, 2, 2048, 2048], P(None, None, 'gx', 'gy')
- seg_residual: float32 [512, 128], P(('gx', 'gy'))
- seg_jvp: float32 [512, 128], P(('gx', 'gy'))
- group_rates: float32 [3, 128], replicated
Inputs may be any that keep to these rules, and one draw needn't show every extreme that they name: perf_cell codes (layer * 128 + xl) * 2048 + row, with xl the column within the strip of 128 columns of the well's block of 32 wells. `parent`: segment 0 of every well names itself; every other segment names a segment of lower number. `group_of`: every group has at least one well.
All inputs are finite; a program needn't handle non-finite values.
Results may differ from a plain program's by a relative error of at most 0.0003.
Values sent between devices are 32-bit elements; how exact they have to be, the bound alone decides.
A program may use at most 128 MiB of HBM per device.

v0:
```python
import jax
import jax.numpy as jnp
from jax import lax
from jax.sharding import PartitionSpec as P

COMPRESS = (0.05, 0.2, 1.0)
VISCOSITY = (0.5, 1.0, 0.2)
DENSITY = (1.0, 0.8, 0.2)
ROCK_COMP = 0.01
GRAVITY = 0.05
UPWIND_WIDTH = 0.02
FRICTION = 0.002
RATE_SCALE = 0.1


def padded_2(x, sides, width):
    for axis, dim in sides:
        devices, length = (lax.axis_size(axis), x.shape[dim])
        up = [(i, (i + 1) % devices) for i in range(devices - 1)]
        down = [(j, i) for i, j in up]
        last = lax.slice_in_dim(x, length - width, length, axis=dim)
        first = lax.slice_in_dim(x, 0, width, axis=dim)
        before = lax.ppermute(last, axis, up)
        after = lax.ppermute(first, axis, down)
        x = jnp.concatenate([before, x, after], axis=dim)
    return x


def phase_props(press, water, gas):
    oil = 1.0 - water - gas
    satur = (water, oil, gas)
    rock = 1.0 + ROCK_COMP * (press - 1.0)
    mobility = []
    masses = []
    for phase in range(3):
        volume = jnp.exp(COMPRESS[phase] * (press - 1.0))
        mobility.append(satur[phase] * satur[phase] * volume / VISCOSITY[phase])
        masses.append(rock * satur[phase] * volume)
    return (jnp.stack(mobility), jnp.stack(masses))


def face_flux(press_in, press_out, mobil_in, mobil_out, trans, lift):
    fluxes = []
    for phase in range(3):
        potential = press_in - press_out + DENSITY[phase] * lift
        upwind = jax.nn.sigmoid(potential / UPWIND_WIDTH)
        fluxes.append(
            trans * (upwind * mobil_in[phase] + (1.0 - upwind) * mobil_out[phase]) * potential
        )
    return jnp.stack(fluxes)


def ancestry(parent):
    count = parent.shape[1]
    segment_ids = jnp.arange(count, dtype=jnp.int32)
    reach = (segment_ids[None, :, None] == segment_ids[None, None, :]) | (
        parent[:, None, :] == segment_ids[None, :, None]
    )
    reach = reach.astype(jnp.bfloat16)
    for level in range((count - 1).bit_length()):
        product = jnp.einsum("wsu,wut->wst", reach, reach, preferred_element_type=jnp.float32)
        reach = jnp.minimum(product, 1.0).astype(jnp.bfloat16)
    return reach.astype(jnp.float32)


def segment_terms(parent, seg_head, well_mode, bhp_limit, target):
    reach = ancestry(parent)

    def equations(total_vals, seg_vals):
        flow = jnp.einsum("wst,wt->ws", reach, total_vals, precision=lax.Precision.HIGHEST)
        above = jnp.take_along_axis(seg_vals, parent, axis=1)
        inner = seg_vals - above - seg_head - FRICTION * flow
        root = jnp.where(
            well_mode == 1, RATE_SCALE * (flow[:, 0] - target), seg_vals[:, 0] - bhp_limit
        )
        return inner.at[:, 0].set(root)

    return equations


def per_device(
    pressure,
    saturations,
    old_mass,
    pore_volume,
    transmissibility,
    direction,
    seg_pressure,
    seg_direction,
    perf_cell,
    well_index,
    parent,
    seg_head,
    well_mode,
    bhp_limit,
    guide_rate,
    group_of,
    group_target,
):
    layers, cols, rows = pressure.shape
    col_count = lax.axis_size("gx")
    row_count = lax.axis_size("gy")
    col_index = lax.axis_index("gx")
    row_index = lax.axis_index("gy")
    col_glob = col_index * cols + jnp.arange(cols, dtype=jnp.int32)
    row_glob = row_index * rows + jnp.arange(rows, dtype=jnp.int32)
    trans_cols = jnp.where(
        (col_glob == cols * col_count - 1)[None, :, None], 0.0, transmissibility[0]
    )
    trans_rows = jnp.where(
        (row_glob == rows * row_count - 1)[None, None, :], 0.0, transmissibility[1]
    )
    stacked = jnp.concatenate(
        [pressure[None], saturations, direction, trans_cols[None], trans_rows[None]], axis=0
    )
    padded = padded_2(stacked, (("gx", 2), ("gy", 3)), 1)
    state_pad = padded[0:3]
    direc_pad = padded[3:6]
    tcol_pad = padded[6]
    trow_pad = padded[7]
    all_rows = rows * row_count
    layer_span = cols * all_rows
    layer = perf_cell // layer_span
    remain = perf_cell % layer_span
    local_row = remain % all_rows - row_index * rows
    owned = (local_row >= 0) & (local_row < rows)
    flat_cell = (layer * cols + remain // all_rows) * rows + jnp.clip(local_row, 0, rows - 1)
    weight = jnp.where(owned, well_index, 0.0)

    def local_terms(state, seg_vals):
        press = state[0]
        mobility, masses = phase_props(press, state[1], state[2])
        mobil_in = mobility[:, :, 1:-1, 1:-1]
        press_in = press[:, 1:-1, 1:-1]
        residual = masses[:, :, 1:-1, 1:-1] * pore_volume - old_mass
        flux_cols = face_flux(
            press[:, :-1, 1:-1],
            press[:, 1:, 1:-1],
            mobility[:, :, :-1, 1:-1],
            mobility[:, :, 1:, 1:-1],
            tcol_pad[:, :-1, 1:-1],
            0.0,
        )
        residual = residual + flux_cols[:, :, 1:] - flux_cols[:, :, :-1]
        flux_rows = face_flux(
            press[:, 1:-1, :-1],
            press[:, 1:-1, 1:],
            mobility[:, :, 1:-1, :-1],
            mobility[:, :, 1:-1, 1:],
            trow_pad[:, 1:-1, :-1],
            0.0,
        )
        residual = residual + flux_rows[:, :, :, 1:] - flux_rows[:, :, :, :-1]
        flux_layers = face_flux(
            press_in[:-1],
            press_in[1:],
            mobil_in[:, :-1],
            mobil_in[:, 1:],
            transmissibility[2][:-1],
            GRAVITY,
        )
        residual = (
            residual
            + jnp.pad(flux_layers, ((0, 0), (0, 1), (0, 0), (0, 0)))
            - jnp.pad(flux_layers, ((0, 0), (1, 0), (0, 0), (0, 0)))
        )
        mobil_flat = mobil_in.reshape(3, -1)
        rates = weight * mobil_flat[:, flat_cell] * (press_in.reshape(-1)[flat_cell] - seg_vals)
        residual = (
            residual.reshape(3, -1)
            .at[:, flat_cell.reshape(-1)]
            .add(rates.reshape(3, -1))
            .reshape(residual.shape)
        )
        return (residual, rates)

    primal, tangent = jax.jvp(local_terms, (state_pad, seg_pressure), (direc_pad, seg_direction))
    cell_residual, rates = primal
    cell_jvp, rate_tangent = tangent
    rate_total = jnp.sum(rates, axis=0)
    total_tangent = jnp.sum(rate_tangent, axis=0)
    member = (
        group_of[:, 0][:, None] == jnp.arange(group_target.shape[0], dtype=jnp.int32)[None, :]
    ).astype(jnp.float32)
    rates_part = jnp.dot(jnp.sum(rates, axis=2), member, precision=lax.Precision.HIGHEST)
    guide_part = jnp.dot(guide_rate, member, precision=lax.Precision.HIGHEST)
    guide_total = lax.psum(guide_part, "gx")
    group_rates = lax.psum(rates_part, ("gx", "gy"))
    target = (
        jnp.dot(member, group_target, precision=lax.Precision.HIGHEST)
        * guide_rate
        / jnp.dot(member, guide_total, precision=lax.Precision.HIGHEST)
    )
    well_count = seg_pressure.shape[0]
    share = well_count // row_count
    start = row_index * share

    def pick(values):
        return lax.dynamic_slice_in_dim(values, start, share, 0)

    total_sum, tangent_sum = lax.psum((rate_total, total_tangent), "gy")
    equations = segment_terms(parent, seg_head, well_mode, bhp_limit, target)
    seg_full, seg_tan = jax.jvp(equations, (total_sum, seg_pressure), (tangent_sum, seg_direction))
    seg_residual = pick(seg_full)
    seg_jvp = pick(seg_tan)
    return (cell_residual, cell_jvp, seg_residual, seg_jvp, group_rates)


def solution(mesh):
    placed = (
        P(None, "gx", "gy"),
        P(None, None, "gx", "gy"),
        P(None, None, "gx", "gy"),
        P(None, "gx", "gy"),
        P(None, None, "gx", "gy"),
        P(None, None, "gx", "gy"),
        P("gx", None),
        P("gx", None),
        P("gx", None),
        P("gx", None),
        P("gx", None),
        P("gx", None),
        P("gx"),
        P("gx"),
        P("gx"),
        P("gx", None),
        P(),
    )
    return jax.shard_map(
        per_device,
        mesh=mesh,
        in_specs=placed,
        out_specs=(
            P(None, None, "gx", "gy"),
            P(None, None, "gx", "gy"),
            P(("gx", "gy"), None),
            P(("gx", "gy"), None),
            P(),
        ),
        check_vma=False,
    )
```

profile of v0, /device:TPU:1, one launch (start us, length us, event | category | flops | bytes accessed | tf_op | source)
XLA Modules:
  0.0 510.7 jit_solution(14686973665699037031)
XLA Ops:
  6.9 4.6 collective-permute-start
  15.0 2.0 minimum_convert_fusion
  17.2 32.3 %psum.29 = f32[128]{0:T(128)S(1)} all-reduce(f32[128]{0:T(128)S(1)} %convolution_bitcast_fusion.1), channel_id=1, replica_groups=mesh['gx'=16,'gy'=16] {'gx'}, use_global_device_ids=true, to_apply=%region_5.6 | all-reduce | flops 128 | bytes 1024 | tf_op jit(solution)/shard_map/psum | solution.py:187
  51.9 9.9 %collective-permute-start.3 = (f32[8,2,130,1]{2,0,3,1:T(8,128)S(1)}, f32[8,2,130,1]{2,0,3,1:T(8,128)S(1)}, u32[]{:S(2)}, u32[]{:S(2)}) collective-permute-start(f32[8,2,130,1]{2,0,3,1:T(8,128)S(1)} %copy.106), channel_id=1, source_target_pairs={{1,0},{2,1},{3,2},{4,3},{5,4},{6,5},{7,6},{8,7},{9,8},{10,9},{11,1... | collective-permute-start | bytes 24968 | tf_op jit(solution)/shard_map/ppermute | solution.py:24
  62.4 3.6 collective-permute-start.2
  66.2 43.2 %gather_fusion.5 = f32[4096]{0:T(1024)} fusion(f32[32,128]{1,0:T(8,128)S(1)} %copy-done.1, s32[4096]{0:T(1024)S(1)} %fusion.156), kind=kCustom, calls=%fused_computation.5 | custom fusion | bytes 65536 | tf_op jit(solution)/shard_map/jvp(jit(take_along_axis))/gather | solution.py:71
  109.4 25.6 %gather_fusion.4 = f32[4096]{0:T(1024)S(1)} fusion(f32[32,128]{1,0:T(8,128)S(1)} %copy-done.2, s32[4096]{0:T(1024)S(1)} %fusion.156), kind=kCustom, calls=%fused_computation.4 | custom fusion | bytes 65536 | tf_op jit(solution)/shard_map/jvp(jit(take_along_axis))/gather | solution.py:71
  145.2 8.6 %copy.109 = f32[3,2,128,128]{0,3,2,1:T(8,128)} copy(f32[3,2,128,128]{3,2,1,0:T(8,128)S(1)} %fusion.34) | data formatting | bytes 786432 | tf_op jit(solution)/shard_map/jvp()/sub | solution.py:163
  153.7 8.5 %copy.110 = f32[3,2,128,128]{0,3,2,1:T(8,128)} copy(f32[3,2,128,128]{3,2,1,0:T(8,128)S(1)} %get-tuple-element.106) | data formatting | bytes 786432 | tf_op jit(solution)/shard_map/jvp()/slice | solution.py:133
  162.2 16.5 %gather_fusion = f32[4096,3]{1,0:T(8,128)S(1)} fusion(f32[3,32768]{0,1:T(8,128)} %bitcast.414, s32[4096]{0:T(1024)S(1)} %get-tuple-element.69), kind=kCustom, calls=%fused_computation | custom fusion | bytes 114688 | tf_op jit(solution)/shard_map/jvp()/gather | solution.py:168
  178.8 40.6 %gather_fusion.3 = f32[4096]{0:T(1024)} fusion(f32[32768]{0:T(1024)S(1)} %bitcast.407, s32[4096]{0:T(1024)S(1)} %get-tuple-element.69), kind=kCustom, calls=%fused_computation.3 | custom fusion | bytes 49152 | tf_op jit(solution)/shard_map/jvp()/gather | solution.py:168
  219.4 23.0 %gather_fusion.1 = f32[4096]{0:T(1024)S(1)} fusion(f32[32768]{0:T(1024)S(1)} %bitcast.408, s32[4096]{0:T(1024)S(1)} %get-tuple-element.69), kind=kCustom, calls=%fused_computation.1 | custom fusion | bytes 49152 | tf_op jit(solution)/shard_map/jvp()/gather | solution.py:168
  242.4 36.5 %scatter_custom_fusion = f32[3,32768]{0,1:T(8,128)} fusion(f32[3,32768]{0,1:T(8,128)} %bitcast.409, s32[4096]{0:T(1024)} %bitcast.429, f32[4096,3]{1,0:T(8,128)S(1)} %gather_fusion, f32[4096]{0:T(1024)S(1)} %bitcast.419, f32[4096]{0:T(1024)S(1)} %bitcast.417), kind=kCustom, calls=%fused_computation.15 | custom fusion | flops 36864 | bytes 475136 | tf_op jit(solution)/shard_map/jvp()/scatter-add | solution.py:172
  278.9 10.7 %copy.115 = f32[3,2,128,128]{3,2,1,0:T(8,128)} copy(f32[3,2,128,128]{0,3,2,1:T(8,128)} %bitcast.410) | data formatting | bytes 786432
  289.6 2.5 fusion.31
  292.1 9.5 %copy.111 = f32[3,2,128,128]{0,3,2,1:T(8,128)} copy(f32[3,2,128,128]{3,2,1,0:T(8,128)} %fusion.31) | data formatting | bytes 786432 | tf_op jit(solution)/shard_map/jvp()/sub | solution.py:163
  301.6 8.5 %copy.112 = f32[3,2,128,128]{0,3,2,1:T(8,128)} copy(f32[3,2,128,128]{3,2,1,0:T(8,128)S(1)} %get-tuple-element.105) | data formatting | bytes 786432 | tf_op jit(solution)/shard_map/jvp()/slice | solution.py:133
  310.1 19.9 %gather_fusion.2 = f32[4096,3]{1,0:T(8,128)} fusion(f32[3,32768]{0,1:T(8,128)} %bitcast.415, s32[4096]{0:T(1024)S(1)} %get-tuple-element.69), kind=kCustom, calls=%fused_computation.2 | custom fusion | bytes 114688 | tf_op jit(solution)/shard_map/jvp()/gather | solution.py:168
  330.1 37.0 %scatter_custom_fusion.1 = f32[3,32768]{0,1:T(8,128)} fusion(f32[3,32768]{0,1:T(8,128)} %bitcast.411, s32[4096]{0:T(1024)} %bitcast.430, f32[4096,3]{1,0:T(8,128)} %gather_fusion.2, f32[4096,3]{1,0:T(8,128)S(1)} %gather_fusion, f32[4096]{0:T(1024)S(1)} %bitcast.425, f32[4096]{0:T(1024)S(1)} %bitcast.420, f32[4096]{0:T(1024)S(1)} %bitcast.418), kind=kCustom, calls=%fused_computation.13 | custom fusion | flops 73728 | bytes 2588672 | tf_op jit(solution)/shard_map/jvp()/scatter-add | solution.py:172
  367.0 10.6 %copy.116 = f32[3,2,128,128]{3,2,1,0:T(8,128)} copy(f32[3,2,128,128]{0,3,2,1:T(8,128)} %bitcast.412) | data formatting | bytes 786432
  377.7 4.6 add_reduce_fusion
  382.4 46.0 %all-reduce.4 = (f32[32,128]{1,0:T(8,128)S(1)}, f32[32,128]{1,0:T(8,128)S(1)}) all-reduce(f32[32,128]{1,0:T(8,128)S(1)} %get-tuple-element.55, f32[32,128]{1,0:T(8,128)S(1)} %get-tuple-element.54), channel_id=1, replica_groups=mesh['gx'=16,'gy'=16] {'gy'}, use_global_device_ids=true, to_apply=%region_3.4 | all-reduce | flops 8192 | bytes 65536 | tf_op jit(solution)/shard_map/psum | solution.py:201
  430.2 1.7 fusion.174
  435.5 75.3 %psum.31 = f32[3,128]{1,0:T(4,128)} all-reduce(f32[3,128]{1,0:T(4,128)S(1)} %fusion.157), channel_id=1, replica_groups=mesh['gx'=16,'gy'=16] {'gx','gy'}, use_global_device_ids=true, to_apply=%region_9.10 | all-reduce | flops 384 | bytes 3072 | tf_op jit(solution)/shard_map/psum | solution.py:188
  (113 shorter events, 28.2 us)
Async XLA Ops:
  0.6 431.5 %copy-start = (f32[128]{0:T(128)S(1)}, f32[128]{0:T(128)}, u32[]{:S(2)}) copy-start(f32[128]{0:T(128)} %param.37) | copy-start | bytes 1540
  0.6 10.9 %copy-start.8 = (s32[32,128]{1,0:T(8,128)S(1)}, s32[32,128]{1,0:T(8,128)}, u32[]{:S(2)}) copy-start(s32[32,128]{1,0:T(8,128)} %param.29) | copy-start | bytes 49156
  0.7 11.5 %copy-start.12 = (f32[32,128]{1,0:T(8,128)S(1)}, f32[32,128]{1,0:T(8,128)}, u32[]{:S(2)}) copy-start(f32[32,128]{1,0:T(8,128)} %param.30) | copy-start | bytes 49156
  0.7 11.5 %copy-start.9 = (s32[32,128]{1,0:T(8,128)S(1)}, s32[32,128]{1,0:T(8,128)}, u32[]{:S(2)}) copy-start(s32[32,128]{1,0:T(8,128)} %param.31) | copy-start | bytes 49156
  5.6 45.2 %collective-permute-start.1 = (f32[8,2,1,128]{3,2,1,0:T(1,128)S(1)}, f32[8,2,1,128]{3,2,1,0:T(1,128)S(1)}, u32[]{:S(2)}, u32[]{:S(2)}) collective-permute-start(f32[8,2,1,128]{3,2,1,0:T(1,128)S(1)} %get-tuple-element.89), channel_id=1, source_target_pairs={{16,0},{32,16},{48,32},{64,48},{80,64},{96,80},{112,96},{128,112},... | collective-permute-start | bytes 24584 | tf_op jit(solution)/shard_map/ppermute | solution.py:24
  6.9 43.9 %collective-permute-start = (f32[8,2,1,128]{3,2,1,0:T(1,128)S(1)}, f32[8,2,1,128]{3,2,1,0:T(1,128)S(1)}, u32[]{:S(2)}, u32[]{:S(2)}) collective-permute-start(f32[8,2,1,128]{3,2,1,0:T(1,128)S(1)} %get-tuple-element.88), channel_id=1, source_target_pairs={{0,16},{16,32},{32,48},{48,64},{64,80},{80,96},{96,112},{112,128},... | collective-permute-start | bytes 24584 | tf_op jit(solution)/shard_map/ppermute | solution.py:23
  15.0 2.0 copy-start.16
  15.0 2.0 copy-start.19
  15.0 35.2 %copy-start.2 = (f32[32,128]{1,0:T(8,128)S(1)}, f32[32,128]{1,0:T(8,128)}, u32[]{:S(2)}) copy-start(f32[32,128]{1,0:T(8,128)} %param.27) | copy-start | bytes 49156
  51.3 14.8 %copy-start.1 = (f32[32,128]{1,0:T(8,128)S(1)}, f32[32,128]{1,0:T(8,128)}, u32[]{:S(2)}) copy-start(f32[32,128]{1,0:T(8,128)} %param.28) | copy-start | bytes 49156
  51.9 83.8 %collective-permute-start.3 = (f32[8,2,130,1]{2,0,3,1:T(8,128)S(1)}, f32[8,2,130,1]{2,0,3,1:T(8,128)S(1)}, u32[]{:S(2)}, u32[]{:S(2)}) collective-permute-start(f32[8,2,130,1]{2,0,3,1:T(8,128)S(1)} %copy.106), channel_id=1, source_target_pairs={{1,0},{2,1},{3,2},{4,3},{5,4},{6,5},{7,6},{8,7},{9,8},{10,9},{11,1... | collective-permute-start | bytes 24968 | tf_op jit(solution)/shard_map/ppermute | solution.py:24
  62.4 73.7 %collective-permute-start.2 = (f32[8,2,130,1]{2,0,3,1:T(8,128)S(1)}, f32[8,2,130,1]{2,0,3,1:T(8,128)S(1)}, u32[]{:S(2)}, u32[]{:S(2)}) collective-permute-start(f32[8,2,130,1]{2,0,3,1:T(8,128)S(1)} %copy.105), channel_id=1, source_target_pairs={{0,1},{1,2},{2,3},{3,4},{4,5},{5,6},{6,7},{7,8},{8,9},{9,10},{10,1... | collective-permute-start | bytes 24968 | tf_op jit(solution)/shard_map/ppermute | solution.py:23
  143.0 1.8 copy-start.6
  219.4 23.0 %copy-start.11 = (f32[4096]{0:T(1024)S(1)}, f32[4096]{0:T(1024)}, u32[]{:S(2)}) copy-start(f32[4096]{0:T(1024)} %gather_fusion.3) | copy-start | bytes 49156
  278.9 10.7 %copy-start.4 = (f32[3,1,128,128]{3,2,1,0:T(8,128)S(1)}, f32[3,1,128,128]{3,2,1,0:T(8,128)}, u32[]{:S(2)}) copy-start(f32[3,1,128,128]{3,2,1,0:T(8,128)} %get-tuple-element.112) | copy-start | bytes 589828
  377.7 50.7 %copy-start.3 = (bf16[32,128,128]{2,1,0:T(8,128)(2,1)S(1)}, bf16[32,128,128]{2,1,0:T(8,128)(2,1)}, u32[]{:S(2)}) copy-start(bf16[32,128,128]{2,1,0:T(8,128)(2,1)} %minimum_convert_fusion) | copy-start | bytes 3145732
  377.7 52.5 %copy-start.10 = (f32[4096]{0:T(1024)S(1)}, f32[4096]{0:T(1024)}, u32[]{:S(2)}) copy-start(f32[4096]{0:T(1024)} %gather_fusion.5) | copy-start | bytes 49156
  382.3 49.8 %copy-start.14 = (f32[32]{0:T(128)S(1)}, f32[32]{0:T(128)}, u32[]{:S(2)}) copy-start(f32[32]{0:T(128)} %slice_reduce_fusion.2) | copy-start | bytes 388
  382.3 49.8 %copy-start.15 = (s32[32]{0:T(128)S(1)}, s32[32]{0:T(128)}, u32[]{:S(2)}) copy-start(s32[32]{0:T(128)} %param.33) | copy-start | bytes 388
  382.3 49.8 %copy-start.17 = (f32[32]{0:T(128)S(1)}, f32[32]{0:T(128)}, u32[]{:S(2)}) copy-start(f32[32]{0:T(128)} %param.35) | copy-start | bytes 388
  382.3 49.8 %copy-start.18 = (f32[32]{0:T(128)S(1)}, f32[32]{0:T(128)}, u32[]{:S(2)}) copy-start(f32[32]{0:T(128)} %param.34) | copy-start | bytes 388
  382.4 49.8 %copy-start.20 = (s32[32,1]{0,1:T(1,128)S(1)}, s32[32,1]{0,1:T(1,128)}, u32[]{:S(2)}) copy-start(s32[32,1]{0,1:T(1,128)} %param.36) | copy-start | bytes 388
  382.4 49.8 %copy-start.21 = (f32[32]{0:T(128)S(1)}, f32[32]{0:T(128)}, u32[]{:S(2)}) copy-start(f32[32]{0:T(128)} %convolution_bitcast_fusion) | copy-start | bytes 388
  382.4 50.1 %copy-start.13 = (f32[32,128]{1,0:T(8,128)S(1)}, f32[32,128]{1,0:T(8,128)}, u32[]{:S(2)}) copy-start(f32[32,128]{1,0:T(8,128)} %param.32) | copy-start | bytes 49156
  (2 other events, 3.0 us)
where the time goes:
time: 512 us; the launch traced here: 511 us
  local copies, waits for them, and re-layouts  233 us (46%)
  blocking collectives  154 us (30%)
  other arithmetic  93.7 us (18%)
  starting transfers between devices  19.4 us (4%)
  matrix products  9.4 us (2%)
    psum x1, blocking collectives, per_device(): group_rates = lax.psum(rates_part, ('gx', 'gy'))  75.3 us
    scatter-add x2, other arithmetic, local_terms(): residual = residual.reshape(3, -1).at[:, flat_cell.reshape(-1)].add(rates...  73.5 us
    gather x2, local copies, waits for them, and re-layouts, equations(): above = jnp.take_along_axis(seg_vals, parent, axis=1)  68.8 us
    gather x2, local copies, waits for them, and re-layouts, local_terms(): press_in.reshape(-1)[flat_cell] - seg_vals  63.6 us
    psum x1, blocking collectives, per_device(): total_sum, tangent_sum = lax.psum((rate_total, total_tangent), 'gy')  46 us
    gather x2, local copies, waits for them, and re-layouts, local_terms(): mobil_flat[:, flat_cell]  36.5 us
    psum x1, blocking collectives, per_device(): guide_total = lax.psum(guide_part, 'gx')  32.3 us
    unnamed x49, local copies, waits for them, and re-layouts  24.4 us
  transfers between devices with their start and end apart: 4, of which 0 were waited for; matrix products, arithmetic and copies ran while one was open for 15% of the time, Pallas kernels for 0%

commit v1 on v0

--- a/solution.py
+++ b/solution.py
@@ -184,7 +184,11 @@
     ).astype(jnp.float32)
     rates_part = jnp.dot(jnp.sum(rates, axis=2), member, precision=lax.Precision.HIGHEST)
     guide_part = jnp.dot(guide_rate, member, precision=lax.Precision.HIGHEST)
-    guide_total = lax.psum(guide_part, "gx")
+    guide_total = guide_part
+    for hop in (1, 2, 4, 8):
+        guide_total = guide_total + lax.ppermute(
+            guide_total, "gx", [(dev, dev ^ hop) for dev in range(16)]
+        )
     group_rates = lax.psum(rates_part, ("gx", "gy"))
     target = (
         jnp.dot(member, group_target, precision=lax.Precision.HIGHEST)

time: 512 us -> 485 us (0.947)
  blocking collectives: 154 us -> 122 us
    psum x1 -> x0, blocking collectives: 32.3 us -> none  [per_device(): guide_total = lax.psum(guide_part, 'gx')]
    gather x2, local copies, waits for them, and re-layouts: 63.6 us -> 46.1 us  [local_terms(): press_in.reshape(-1)[flat_cell] - seg_vals]
    gather x2, local copies, waits for them, and re-layouts: 68.8 us -> 86.3 us  [equations(): above = jnp.take_along_axis(seg_vals, parent, axis=1)]
    ppermute x0 -> x4, starting transfers between devices: none -> 9.12 us  [per_device(): lax.ppermute(guide_total, 'gx', [(dev, dev ^ hop) for dev in range(16)])]
    ppermute x2, starting transfers between devices: 11.2 us -> 5 us  [padded_2(): after = lax.ppermute(first, axis, down)]
    unnamed x49 -> x55, local copies, waits for them, and re-layouts: 24.4 us -> 24.4 us
  transfers between devices with their start and end apart: 4 -> 8, of which waited for: 0 -> 0; matrix products, arithmetic and copies ran while one was open for 15% -> 68% of each run, Pallas kernels for 0% -> 0%
where the time goes in v1:
time: 485 us; the launch traced here: 484 us
  local copies, waits for them, and re-layouts  232 us (48%)
  blocking collectives  122 us (25%)
  other arithmetic  94.2 us (19%)
  starting transfers between devices  22.1 us (5%)
  matrix products  11.6 us (2%)
    gather x2, local copies, waits for them, and re-layouts, equations(): above = jnp.take_along_axis(seg_vals, parent, axis=1)  86.3 us
    psum x1, blocking collectives, per_device(): group_rates = lax.psum(rates_part, ('gx', 'gy'))  76.2 us
    scatter-add x2, other arithmetic, local_terms(): residual = residual.reshape(3, -1).at[:, flat_cell.reshape(-1)].add(rates...  73.5 us
    gather x2, local copies, waits for them, and re-layouts, local_terms(): press_in.reshape(-1)[flat_cell] - seg_vals  46.1 us
    psum x1, blocking collectives, per_device(): total_sum, tangent_sum = lax.psum((rate_total, total_tangent), 'gy')  45.8 us
    gather x2, local copies, waits for them, and re-layouts, local_terms(): mobil_flat[:, flat_cell]  36.5 us
    unnamed x55, local copies, waits for them, and re-layouts  24.4 us
    slice x2, local copies, waits for them, and re-layouts, local_terms(): mobil_in = mobility[:, :, 1:-1, 1:-1]  17.2 us
  transfers between devices with their start and end apart: 8, of which 0 were waited for; matrix products, arithmetic and copies ran while one was open for 68% of the time, Pallas kernels for 0%

profile of v1, /device:TPU:1, one launch (start us, length us, event | category | flops | bytes accessed | tf_op | source)
XLA Modules:
  0.0 483.5 jit_solution(9208708360591758359)
XLA Ops:
  6.9 4.6 collective-permute-start
  16.7 2.0 minimum_convert_fusion
  19.5 4.6 collective-permute-start.5
  25.2 3.7 collective-permute-start.3
  29.6 3.5 collective-permute-start.2
  33.1 43.2 %gather_fusion.5 = f32[4096]{0:T(1024)} fusion(f32[32,128]{1,0:T(8,128)S(1)} %copy-done.2, s32[4096]{0:T(1024)S(1)} %fusion.156), kind=kCustom, calls=%fused_computation.5 | custom fusion | bytes 65536 | tf_op jit(solution)/shard_map/jvp(jit(take_along_axis))/gather | solution.py:71
  77.7 43.1 %gather_fusion.4 = f32[4096]{0:T(1024)} fusion(f32[32,128]{1,0:T(8,128)S(1)} %copy-done.3, s32[4096]{0:T(1024)S(1)} %fusion.156), kind=kCustom, calls=%fused_computation.4 | custom fusion | bytes 65536 | tf_op jit(solution)/shard_map/jvp(jit(take_along_axis))/gather | solution.py:71
  134.0 8.6 %copy.109 = f32[3,2,128,128]{0,3,2,1:T(8,128)} copy(f32[3,2,128,128]{3,2,1,0:T(8,128)S(1)} %fusion.34) | data formatting | bytes 786432 | tf_op jit(solution)/shard_map/jvp()/sub | solution.py:163
  142.6 8.6 %copy.110 = f32[3,2,128,128]{0,3,2,1:T(8,128)} copy(f32[3,2,128,128]{3,2,1,0:T(8,128)S(1)} %get-tuple-element.106) | data formatting | bytes 786432 | tf_op jit(solution)/shard_map/jvp()/slice | solution.py:133
  151.2 16.5 %gather_fusion = f32[4096,3]{1,0:T(8,128)S(1)} fusion(f32[3,32768]{0,1:T(8,128)} %bitcast.414, s32[4096]{0:T(1024)S(1)} %get-tuple-element.69), kind=kCustom, calls=%fused_computation | custom fusion | bytes 114688 | tf_op jit(solution)/shard_map/jvp()/gather | solution.py:168
  167.7 23.0 %gather_fusion.3 = f32[4096]{0:T(1024)S(1)} fusion(f32[32768]{0:T(1024)S(1)} %bitcast.407, s32[4096]{0:T(1024)S(1)} %get-tuple-element.69), kind=kCustom, calls=%fused_computation.3 | custom fusion | bytes 49152 | tf_op jit(solution)/shard_map/jvp()/gather | solution.py:168
  190.8 23.0 %gather_fusion.1 = f32[4096]{0:T(1024)S(1)} fusion(f32[32768]{0:T(1024)S(1)} %bitcast.408, s32[4096]{0:T(1024)S(1)} %get-tuple-element.69), kind=kCustom, calls=%fused_computation.1 | custom fusion | bytes 49152 | tf_op jit(solution)/shard_map/jvp()/gather | solution.py:168
  213.8 8.6 %copy.112 = f32[3,2,128,128]{0,3,2,1:T(8,128)} copy(f32[3,2,128,128]{3,2,1,0:T(8,128)S(1)} %get-tuple-element.105) | data formatting | bytes 786432 | tf_op jit(solution)/shard_map/jvp()/slice | solution.py:133
  222.4 19.9 %gather_fusion.2 = f32[4096,3]{1,0:T(8,128)} fusion(f32[3,32768]{0,1:T(8,128)} %bitcast.415, s32[4096]{0:T(1024)S(1)} %get-tuple-element.69), kind=kCustom, calls=%fused_computation.2 | custom fusion | bytes 114688 | tf_op jit(solution)/shard_map/jvp()/gather | solution.py:168
  242.4 5.2 %add_reduce_fusion = (f32[32,128]{1,0:T(8,128)S(1)}, f32[32,128]{1,0:T(8,128)S(1)}, f32[3,32]{0,1:T(8,128)}) fusion(f32[3,32,128]{0,2,1:T(8,128)} %bitcast.416, f32[3,32,128]{0,2,1:T(8,128)S(1)} %bitcast.413, f32[32,128]{1,0:T(8,128)S(1)} %get-tuple-element.113, f32[32,128]{1,0:T(8,128)S(1)} %get-tuple-element.114, f32[32,128]{1,0:T(8,128)S(1)} %and_select_fusion, ...), kind=kLoop, calls=%fused_computation.17 | loop fusion | flops 126880 | bytes 229760 | tf_op jit(solution)/shard_map/reduce_sum | solution.py:181
  247.6 45.8 %all-reduce.4 = (f32[32,128]{1,0:T(8,128)}, f32[32,128]{1,0:T(8,128)}) all-reduce(f32[32,128]{1,0:T(8,128)S(1)} %get-tuple-element.55, f32[32,128]{1,0:T(8,128)S(1)} %get-tuple-element.54), channel_id=1, replica_groups=mesh['gx'=16,'gy'=16] {'gy'}, use_global_device_ids=true, to_apply=%region_3.4 | all-reduce | flops 8192 | bytes 65536 | tf_op jit(solution)/shard_map/psum | solution.py:205
  293.4 2.6 fusion.174
  296.9 2.4 fusion.173
  299.8 36.5 %scatter_custom_fusion = f32[3,32768]{0,1:T(8,128)} fusion(f32[3,32768]{0,1:T(8,128)} %bitcast.409, s32[4096]{0:T(1024)} %bitcast.429, f32[4096,3]{1,0:T(8,128)S(1)} %gather_fusion, f32[4096]{0:T(1024)S(1)} %bitcast.419, f32[4096]{0:T(1024)S(1)} %bitcast.417), kind=kCustom, calls=%fused_computation.15 | custom fusion | flops 36864 | bytes 475136 | tf_op jit(solution)/shard_map/jvp()/scatter-add | solution.py:172
  336.3 10.6 %copy.115 = f32[3,2,128,128]{3,2,1,0:T(8,128)} copy(f32[3,2,128,128]{0,3,2,1:T(8,128)} %bitcast.410) | data formatting | bytes 786432
  346.9 8.6 %copy.111 = f32[3,2,128,128]{0,3,2,1:T(8,128)} copy(f32[3,2,128,128]{3,2,1,0:T(8,128)S(1)} %fusion.31) | data formatting | bytes 786432 | tf_op jit(solution)/shard_map/jvp()/sub | solution.py:163
  355.5 37.0 %scatter_custom_fusion.1 = f32[3,32768]{0,1:T(8,128)} fusion(f32[3,32768]{0,1:T(8,128)} %bitcast.411, s32[4096]{0:T(1024)} %bitcast.430, f32[4096,3]{1,0:T(8,128)} %gather_fusion.2, f32[4096,3]{1,0:T(8,128)S(1)} %gather_fusion, f32[4096]{0:T(1024)S(1)} %bitcast.425, f32[4096]{0:T(1024)S(1)} %bitcast.420, f32[4096]{0:T(1024)S(1)} %bitcast.418), kind=kCustom, calls=%fused_computation.13 | custom fusion | flops 73728 | bytes 2588672 | tf_op jit(solution)/shard_map/jvp()/scatter-add | solution.py:172
  392.6 10.7 %copy.116 = f32[3,2,128,128]{3,2,1,0:T(8,128)} copy(f32[3,2,128,128]{0,3,2,1:T(8,128)} %bitcast.412) | data formatting | bytes 786432
  407.3 76.2 %psum.23 = f32[3,128]{1,0:T(4,128)} all-reduce(f32[3,128]{1,0:T(4,128)S(1)} %fusion.157), channel_id=1, replica_groups=mesh['gx'=16,'gy'=16] {'gx','gy'}, use_global_device_ids=true, to_apply=%region_8.9 | all-reduce | flops 384 | bytes 3072 | tf_op jit(solution)/shard_map/psum | solution.py:192
  (129 shorter events, 33.6 us)
Async XLA Ops:
  0.6 18.0 %copy-start = (f32[128]{0:T(128)S(1)}, f32[128]{0:T(128)}, u32[]{:S(2)}) copy-start(f32[128]{0:T(128)} %param.37) | copy-start | bytes 1540
  0.7 10.9 %copy-start.21 = (f32[32]{0:T(128)S(1)}, f32[32]{0:T(128)}, u32[]{:S(2)}) copy-start(f32[32]{0:T(128)} %param.35) | copy-start | bytes 388
  0.7 10.9 %copy-start.23 = (s32[32,1]{0,1:T(1,128)S(1)}, s32[32,1]{0,1:T(1,128)}, u32[]{:S(2)}) copy-start(s32[32,1]{0,1:T(1,128)} %param.36) | copy-start | bytes 388
  0.7 12.5 %copy-start.14 = (s32[32,128]{1,0:T(8,128)S(1)}, s32[32,128]{1,0:T(8,128)}, u32[]{:S(2)}) copy-start(s32[32,128]{1,0:T(8,128)} %param.29) | copy-start | bytes 49156
  0.7 13.2 %copy-start.18 = (f32[32,128]{1,0:T(8,128)S(1)}, f32[32,128]{1,0:T(8,128)}, u32[]{:S(2)}) copy-start(f32[32,128]{1,0:T(8,128)} %param.30) | copy-start | bytes 49156
  0.7 13.2 %copy-start.15 = (s32[32,128]{1,0:T(8,128)S(1)}, s32[32,128]{1,0:T(8,128)}, u32[]{:S(2)}) copy-start(s32[32,128]{1,0:T(8,128)} %param.31) | copy-start | bytes 49156
  5.6 18.5 %collective-permute-start.1 = (f32[8,2,1,128]{3,2,1,0:T(1,128)S(1)}, f32[8,2,1,128]{3,2,1,0:T(1,128)S(1)}, u32[]{:S(2)}, u32[]{:S(2)}) collective-permute-start(f32[8,2,1,128]{3,2,1,0:T(1,128)S(1)} %get-tuple-element.89), channel_id=1, source_target_pairs={{16,0},{32,16},{48,32},{64,48},{80,64},{96,80},{112,96},{128,112},... | collective-permute-start | bytes 24584 | tf_op jit(solution)/shard_map/ppermute | solution.py:24
  6.9 17.2 %collective-permute-start = (f32[8,2,1,128]{3,2,1,0:T(1,128)S(1)}, f32[8,2,1,128]{3,2,1,0:T(1,128)S(1)}, u32[]{:S(2)}, u32[]{:S(2)}) collective-permute-start(f32[8,2,1,128]{3,2,1,0:T(1,128)S(1)} %get-tuple-element.88), channel_id=1, source_target_pairs={{0,16},{16,32},{32,48},{48,64},{64,80},{80,96},{96,112},{112,128},... | collective-permute-start | bytes 24584 | tf_op jit(solution)/shard_map/ppermute | solution.py:23
  11.7 7.8 %collective-permute-start.4 = (f32[128]{0:T(128)S(1)}, f32[128]{0:T(128)S(1)}, u32[]{:S(2)}, u32[]{:S(2)}) collective-permute-start(f32[128]{0:T(128)S(1)} %convolution_bitcast_fusion.1), channel_id=1, source_target_pairs={{0,16},{16,0},{32,48},{48,32},{64,80},{80,64},{96,112},{112,96},{1... | collective-permute-start | bytes 1544 | tf_op jit(solution)/shard_map/ppermute | solution.py:189
  19.5 56.8 %collective-permute-start.5 = (f32[128]{0:T(128)S(1)}, f32[128]{0:T(128)S(1)}, u32[]{:S(2)}, u32[]{:S(2)}) collective-permute-start(f32[128]{0:T(128)S(1)} %add.278), channel_id=1, source_target_pairs={{0,32},{16,48},{32,0},{48,16},{64,96},{80,112},{96,64},{112,80},{1... | collective-permute-start | bytes 1544 | tf_op jit(solution)/shard_map/ppermute | solution.py:189
  24.6 8.4 %copy-start.2 = (f32[32,128]{1,0:T(8,128)S(1)}, f32[32,128]{1,0:T(8,128)}, u32[]{:S(2)}) copy-start(f32[32,128]{1,0:T(8,128)} %param.28) | copy-start | bytes 49156
  25.2 98.4 %collective-permute-start.3 = (f32[8,2,130,1]{2,0,3,1:T(8,128)S(1)}, f32[8,2,130,1]{2,0,3,1:T(8,128)S(1)}, u32[]{:S(2)}, u32[]{:S(2)}) collective-permute-start(f32[8,2,130,1]{2,0,3,1:T(8,128)S(1)} %copy.106), channel_id=1, source_target_pairs={{1,0},{2,1},{3,2},{4,3},{5,4},{6,5},{7,6},{8,7},{9,8},{10,9},{11,1... | collective-permute-start | bytes 24968 | tf_op jit(solution)/shard_map/ppermute | solution.py:24
  29.6 94.5 %collective-permute-start.2 = (f32[8,2,130,1]{2,0,3,1:T(8,128)S(1)}, f32[8,2,130,1]{2,0,3,1:T(8,128)S(1)}, u32[]{:S(2)}, u32[]{:S(2)}) collective-permute-start(f32[8,2,130,1]{2,0,3,1:T(8,128)S(1)} %copy.105), channel_id=1, source_target_pairs={{0,1},{1,2},{2,3},{3,4},{4,5},{5,6},{6,7},{7,8},{8,9},{9,10},{10,1... | collective-permute-start | bytes 24968 | tf_op jit(solution)/shard_map/ppermute | solution.py:23
  76.3 45.2 %collective-permute-start.6 = (f32[128]{0:T(128)S(1)}, f32[128]{0:T(128)S(1)}, u32[]{:S(2)}, u32[]{:S(2)}) collective-permute-start(f32[128]{0:T(128)S(1)} %add.279), channel_id=1, source_target_pairs={{0,64},{16,80},{32,96},{48,112},{64,0},{80,16},{96,32},{112,48},{1... | collective-permute-start | bytes 1544 | tf_op jit(solution)/shard_map/ppermute | solution.py:189
  122.0 281.2 %collective-permute-start.7 = (f32[128]{0:T(128)}, f32[128]{0:T(128)}, u32[]{:S(2)}, u32[]{:S(2)}) collective-permute-start(f32[128]{0:T(128)} %add.280), channel_id=1, source_target_pairs={{0,128},{16,144},{32,160},{48,176},{64,192},{80,208},{96,224},{112... | collective-permute-start | bytes 1544 | tf_op jit(solution)/shard_map/ppermute | solution.py:189
  242.4 51.1 %copy-start.4 = (bf16[32,128,128]{2,1,0:T(8,128)(2,1)S(1)}, bf16[32,128,128]{2,1,0:T(8,128)(2,1)}, u32[]{:S(2)}) copy-start(bf16[32,128,128]{2,1,0:T(8,128)(2,1)} %minimum_convert_fusion) | copy-start | bytes 3145732
  293.4 6.1 %copy-start.9 = (f32[3,1,128,128]{3,2,1,0:T(8,128)S(1)}, f32[3,1,128,128]{3,2,1,0:T(8,128)}, u32[]{:S(2)}) copy-start(f32[3,1,128,128]{3,2,1,0:T(8,128)} %get-tuple-element.112) | copy-start | bytes 589828
  392.5 10.8 %copy-start.20 = (s32[32]{0:T(128)S(1)}, s32[32]{0:T(128)}, u32[]{:S(2)}) copy-start(s32[32]{0:T(128)} %param.33) | copy-start | bytes 388
  392.5 10.8 %copy-start.22 = (f32[32]{0:T(128)S(1)}, f32[32]{0:T(128)}, u32[]{:S(2)}) copy-start(f32[32]{0:T(128)} %param.34) | copy-start | bytes 388
  392.5 10.8 %copy-start.24 = (f32[32]{0:T(128)S(1)}, f32[32]{0:T(128)}, u32[]{:S(2)}) copy-start(f32[32]{0:T(128)} %fusion.14) | copy-start | bytes 388
  392.5 11.7 %copy-start.16 = (f32[4096]{0:T(1024)S(1)}, f32[4096]{0:T(1024)}, u32[]{:S(2)}) copy-start(f32[4096]{0:T(1024)} %gather_fusion.4) | copy-start | bytes 49156
  392.5 11.7 %copy-start.19 = (f32[32,128]{1,0:T(8,128)S(1)}, f32[32,128]{1,0:T(8,128)}, u32[]{:S(2)}) copy-start(f32[32,128]{1,0:T(8,128)} %param.32) | copy-start | bytes 49156
  392.5 14.5 %copy-start.17 = (f32[3,32]{0,1:T(8,128)S(1)}, f32[3,32]{0,1:T(8,128)}, u32[]{:S(2)}) copy-start(f32[3,32]{0,1:T(8,128)} %get-tuple-element.56) | copy-start | bytes 1156
  392.5 91.0 %copy-start.1 = (f32[128]{0:T(128)S(1)}, f32[128]{0:T(128)}, u32[]{:S(2)}) copy-start(f32[128]{0:T(128)} %param.37) | copy-start | bytes 1540
  (9 other events, 39.5 us)
